TPU v7x, 32 devices: a whole 2x2x4 slice. The times are simulated.
32 devices in a mesh: groups: 2 (over y), pipe: 4 (over z), hour: 2 (over x), seg: 2 (over core).
Axes of the slice: x: 2, y: 2, z: 4, core: 2. Of those that a mesh axis runs over, the one named last changes fastest.
Arguments:
- segment_flow: float32 [16, 64, 1024], P(('groups', 'hour'), 'seg', 'pipe'), parts along dimension 0, may hold values from -4 to 4
- linepack: float32 [16, 64, 1024], P(('groups', 'hour'), 'seg', 'pipe'), parts along dimension 0, may hold values from 0.2 to 2.4
- mass_dual: float32 [16, 64, 1024], P(('groups', 'hour'), 'seg', 'pipe'), parts along dimension 0, may hold values from -3 to 3
- momentum_dual: float32 [16, 64, 1024], P(('groups', 'hour'), 'seg', 'pipe'), parts along dimension 0, may hold values from -3 to 3
- contract_dual: float32 [16, 2, 32, 128], P(('groups', 'hour'), 'seg', 'pipe'), parts along dimension 0, may hold values from -3 to 3
- flow_cost: float32 [16, 64, 1024], P(('groups', 'hour'), 'seg', 'pipe'), parts along dimension 0, may hold values from -24 to 24
- injection: float32 [16, 64, 1024], P(('groups', 'hour'), 'seg', 'pipe'), parts along dimension 0, may hold values from -3 to 3
- contract_target: float32 [16, 2, 32, 128], P(('groups', 'hour'), 'seg', 'pipe'), parts along dimension 0, may hold values from 0.4 to 2
- friction_table: float32 [16], replicated, may hold values from 0.3 to 3
- friction_class: int32 [64, 2048], P('seg', ('groups', 'pipe')), parts along dimension 1, may hold values from 0 to 15
- matching: int32 [2048], P('groups'), parts along dimension 0, may hold values from 0 to 1023, as said below
- contract_map: int32 [16, 1024], P(('groups', 'hour')), parts along dimension 0, may hold values from 0 to 127
Outputs:
- flow_final: float32 [16, 64, 1024], P(('groups', 'hour'), 'seg', 'pipe'), parts along dimension 0
- linepack_final: float32 [16, 64, 1024], P(('groups', 'hour'), 'seg', 'pipe'), parts along dimension 0
- mass_dual_final: float32 [16, 64, 1024], P(('groups', 'hour'), 'seg', 'pipe'), parts along dimension 0
- momentum_dual_final: float32 [16, 64, 1024], P(('groups', 'hour'), 'seg', 'pipe'), parts along dimension 0
- contract_dual_final: float32 [16, 2, 32, 128], P(('groups', 'hour'), 'seg', 'pipe'), parts along dimension 0
- primal_weight: float32 [2], P('groups'), parts along dimension 0
There are 2 independent parts, one for each index of `groups`. A program takes and returns all parts, laid end to end along the dimension named above; an argument that names none is the same for every part. Nothing has to cross between parts.
Inputs may be any that keep to these rules, and one draw needn't show every extreme that they name: `matching`: every pipe's inlet is fed by the outlet of exactly one pipe: each number of 0 to 1023 appears once; for any two blocks of 256 consecutive pipes, exactly 64 pipes of the first are fed from outlets of the second.
All inputs are finite; a program needn't handle non-finite values.
Results may differ from a plain program's by a relative error of at most 0.0001.
Values sent between devices are 32-bit elements; how exact they have to be, the bound alone decides.
A program may use at most 64 MiB of HBM per device.

v0:
```python
import math
import jax
import jax.numpy as jnp
from jax import lax
from jax.sharding import PartitionSpec as P

ITERS = 2
FLOW_CAP = 1.5
PACK_CAP = 2.5
STEP_SCALE = 0.25
NORM_EPS = 1e-06


def padded(cells, sides, width):
    for axis, dim in sides:
        count = lax.axis_size(axis)
        ends = count - 1
        head = lax.slice_in_dim(cells, 0, width, axis=dim)
        tail = lax.slice_in_dim(cells, cells.shape[dim] - width, cells.shape[dim], axis=dim)
        cells = jnp.concatenate(
            [
                lax.ppermute(tail, axis, [(i, (i + 1) % count) for i in range(ends)]),
                cells,
                lax.ppermute(head, axis, [((i + 1) % count, i) for i in range(ends)]),
            ],
            axis=dim,
        )
    return cells


def widened_pair(stacked):
    return padded(stacked, (("hour", 1), ("seg", 2)), 1)


def other_half(edge_row, half_index, partner_local):
    gathered = lax.all_gather(edge_row[:, None, :], ("pipe", "seg"), axis=1, tiled=True)
    hour_rows, row_count, row_width = gathered.shape
    seg_count = lax.axis_size("seg")
    picked = gathered.reshape(hour_rows, row_count // seg_count, seg_count, row_width)[
        :, :, half_index, :
    ]
    far_rows = picked.reshape(hour_rows, row_count // seg_count * row_width)
    return jnp.take(far_rows, partner_local, axis=1)


def contract_local(values, contract_rows, class_count):
    hour_rows, seg_rows, pipe_rows = values.shape
    block = math.gcd(pipe_rows, 2048)
    classes = jnp.arange(class_count, dtype=jnp.int32)

    def add_block(block_index, total):
        partial_value = lax.dynamic_slice_in_dim(values, block_index * block, block, 2)
        row_map = lax.dynamic_slice_in_dim(contract_rows, block_index * block, block, 1)
        onehot = (row_map[:, :, None] == classes[None, None, :]).astype(jnp.float32)
        return total + jnp.einsum(
            "hsp,hpc->hsc",
            partial_value,
            onehot,
            precision=lax.Precision.HIGHEST,
            preferred_element_type=jnp.float32,
        )

    return lax.fori_loop(
        0, pipe_rows // block, add_block, jnp.zeros((hour_rows, seg_rows, class_count), jnp.float32)
    )


def spread_local(duals, contract_rows):
    hour_rows, seg_rows, class_count = duals.shape
    pipe_rows = contract_rows.shape[1]
    block = math.gcd(pipe_rows, 2048)
    classes = jnp.arange(class_count, dtype=jnp.int32)

    def fill_block(block_index, result_now):
        row_map = lax.dynamic_slice_in_dim(contract_rows, block_index * block, block, 1)
        onehot = (row_map[:, :, None] == classes[None, None, :]).astype(jnp.float32)
        partial_value = jnp.einsum(
            "hsc,hpc->hsp",
            duals,
            onehot,
            precision=lax.Precision.HIGHEST,
            preferred_element_type=jnp.float32,
        )
        return lax.dynamic_update_slice_in_dim(result_now, partial_value, block_index * block, 2)

    return lax.fori_loop(
        0, pipe_rows // block, fill_block, jnp.zeros((hour_rows, seg_rows, pipe_rows), jnp.float32)
    )


def on_device(
    segment_flow,
    linepack,
    mass_dual,
    momentum_dual,
    contract_dual,
    flow_cost,
    injection,
    contract_target,
    friction_table,
    friction_class,
    matching,
    contract_map,
):
    hour_rows, seg_rows, pipe_rows = segment_flow.shape
    class_count = contract_dual.shape[3]
    pipe_count = lax.axis_size("pipe")
    total_pipes = pipe_rows * pipe_count
    share_scale = class_count / total_pipes
    pipe_start = lax.axis_index("pipe") * pipe_rows
    seg_index = lax.axis_index("seg")
    at_start = seg_index == 0
    at_end = seg_index == lax.axis_size("seg") - 1
    levels = jnp.arange(friction_table.shape[0], dtype=jnp.int32)
    friction = jnp.sum(
        jnp.where(
            friction_class[None] == levels[:, None, None], friction_table[:, None, None], 0.0
        ),
        axis=0,
    )[None]
    inverse = (
        jnp.zeros_like(matching).at[matching].set(jnp.arange(matching.shape[0], dtype=jnp.int32))
    )
    source_local = lax.dynamic_slice_in_dim(matching, pipe_start, pipe_rows)
    target_local = lax.dynamic_slice_in_dim(inverse, pipe_start, pipe_rows)
    contract_now = contract_dual.reshape(hour_rows, contract_dual.shape[2], class_count)
    target_now = contract_target.reshape(hour_rows, contract_target.shape[2], class_count)
    weight = jnp.float32(1.0)
    for iteration in range(ITERS):
        primal_step = STEP_SCALE / weight
        dual_step = STEP_SCALE * weight
        widened = widened_pair(jnp.stack([mass_dual, momentum_dual]))
        last_base = widened[0, 1:-1, -1, :]
        later_hour = widened[0, 2:, 1:-1, :]
        before_seg = widened[1, 1:-1, :-2, :]
        returned = other_half(mass_dual[:, 0, :], 0, target_local)
        last_row = last_base + jnp.where(at_end, returned, 0.0)
        next_seg = jnp.concatenate([mass_dual[:, 1:, :], last_row[:, None, :]], axis=1)
        grad_flow = mass_dual - next_seg + friction * momentum_dual
        hour_spread = spread_local(contract_now, contract_map)
        spread = lax.all_to_all(hour_spread, "pipe", split_axis=2, concat_axis=1, tiled=True)
        grad_pack = mass_dual - later_hour - momentum_dual + before_seg + share_scale * spread
        grad_flow, grad_pack = (grad_flow, grad_pack)
        flow_next = jnp.clip(
            segment_flow - primal_step * (flow_cost - grad_flow), -FLOW_CAP, FLOW_CAP
        )
        pack_next = jnp.clip(linepack + primal_step * grad_pack, 0.0, PACK_CAP)
        flow_bar = 2.0 * flow_next - segment_flow
        pack_bar = 2.0 * pack_next - linepack
        forward_widened = widened_pair(jnp.stack([flow_bar, pack_bar]))
        first_base = forward_widened[0, 1:-1, 0, :]
        earlier = forward_widened[1, :-2, 1:-1, :]
        after_seg = forward_widened[1, 1:-1, 2:, :]
        inflow = other_half(flow_bar[:, -1, :], 1, source_local)
        first_row = first_base + jnp.where(at_start, inflow, 0.0)
        upstream = jnp.concatenate([first_row[:, None, :], flow_bar[:, :-1, :]], axis=1)
        mass_rows = pack_bar - earlier + flow_bar - upstream
        momentum = friction * flow_bar - (pack_bar - after_seg)
        hour_major = lax.all_to_all(pack_bar, "pipe", split_axis=1, concat_axis=2, tiled=True)
        totals = contract_local(hour_major, contract_map, class_count)
        mass_rows, momentum, totals = (mass_rows, momentum, share_scale * totals)
        mass_next = mass_dual + dual_step * (injection - mass_rows)
        momentum_next = momentum_dual - dual_step * momentum
        contract_next = contract_now + dual_step * (target_now - totals)
        primal_sq = jnp.sum((flow_next - segment_flow) ** 2) + jnp.sum((pack_next - linepack) ** 2)
        dual_sq = (
            jnp.sum((mass_next - mass_dual) ** 2)
            + jnp.sum((momentum_next - momentum_dual) ** 2)
            + jnp.sum((contract_next - contract_now) ** 2)
        )
        primal_total, dual_total = lax.psum((primal_sq, dual_sq), ("pipe", "hour", "seg"))
        weight = jnp.sqrt(weight * jnp.sqrt((dual_total + NORM_EPS) / (primal_total + NORM_EPS)))
        segment_flow, linepack = (flow_next, pack_next)
        mass_dual, momentum_dual, contract_now = (mass_next, momentum_next, contract_next)
    return (
        segment_flow,
        linepack,
        mass_dual,
        momentum_dual,
        contract_now.reshape(contract_dual.shape),
        weight.reshape(1),
    )


def solution(mesh):
    return jax.shard_map(
        on_device,
        mesh=mesh,
        in_specs=(
            P(("groups", "hour"), "seg", "pipe"),
            P(("groups", "hour"), "seg", "pipe"),
            P(("groups", "hour"), "seg", "pipe"),
            P(("groups", "hour"), "seg", "pipe"),
            P(("groups", "hour"), "seg", "pipe", None),
            P(("groups", "hour"), "seg", "pipe"),
            P(("groups", "hour"), "seg", "pipe"),
            P(("groups", "hour"), "seg", "pipe", None),
            P(),
            P("seg", ("groups", "pipe")),
            P("groups"),
            P(("groups", "hour"), None),
        ),
        out_specs=(
            P(("groups", "hour"), "seg", "pipe"),
            P(("groups", "hour"), "seg", "pipe"),
            P(("groups", "hour"), "seg", "pipe"),
            P(("groups", "hour"), "seg", "pipe"),
            P(("groups", "hour"), "seg", "pipe", None),
            P("groups"),
        ),
        check_vma=False,
    )
```

profile of v0, /device:TPU:0, one launch (start us, length us, event | category | flops | bytes accessed | tf_op | source)
XLA Modules:
  0.0 255.9 jit_solution(9958504613072737630)
XLA Ops:
  3.7 3.1 %reshape.116 = f32[4,1,8192]{2,1,0:T(1,128)} reshape(f32[1024,4,8]{2,1,0:T(4,128)S(1)} %bitcast.195) | data formatting | bytes 262144
  6.8 6.3 %all-to-all-start = ((f32[4,1,8192]{2,1,0:T(1,128)}), f32[4,1,8192]{2,1,0:T(1,128)S(1)}, u32[]{:S(2)}, u32[]{:S(2)}) async-start(f32[4,1,8192]{2,1,0:T(1,128)} %reshape.116), calls=%async_computation | async-start | bytes 262144 | tf_op jit(solution)/shard_map/all_to_all | solution.py:141
  14.5 4.5 %collective-permute-start = (f32[2,1,32,256]{3,2,1,0:T(8,128)S(1)}, f32[2,1,32,256]{3,2,1,0:T(8,128)S(1)}, u32[]{:S(2)}, u32[]{:S(2)}) collective-permute-start(f32[2,1,32,256]{3,2,1,0:T(8,128)S(1)} %get-tuple-element.135), channel_id=1, source_target_pairs={{0,2},{1,3},{4,6},{5,7},{8,10},{9,11},{12,14},{13,15},{16,18},{17,... | collective-permute-start | bytes 196616 | tf_op jit(solution)/shard_map/ppermute | solution.py:22
  19.1 14.6 %all_gather.12 = f32[4,8,256]{2,0,1:T(4,128)S(1)} all-gather(f32[4,1,256]{2,0,1:T(4,128)S(1)} %copy.255), channel_id=1, replica_groups=mesh['groups'=2,'pipe'=4,'hour'=2,'seg'=2] {'pipe','seg'}, dimensions={1}, use_global_device_ids=true | all-gather | bytes 36864 | tf_op jit(solution)/shard_map/all_gather | solution.py:36
  33.9 4.3 %scatter_custom_fusion = s32[1024]{0:T(1024)S(1)} fusion(s32[1024]{0:T(1024)S(1)} %compare_select_fusion, s32[1024]{0:T(1024)S(1)} %iota.14, s32[]{:T(128)} %constant.26.clone.1), kind=kCustom, calls=%fused_computation.140 | custom fusion | bytes 4100 | tf_op jit(solution)/shard_map/scatter | solution.py:122
  40.3 2.2 collective-permute-start.3
  47.8 2.5 reshape.117
  58.7 4.5 %collective-permute-start.4 = (f32[2,1,32,256]{3,2,1,0:T(8,128)S(1)}, f32[2,1,32,256]{3,2,1,0:T(8,128)S(1)}, u32[]{:S(2)}, u32[]{:S(2)}) collective-permute-start(f32[2,1,32,256]{3,2,1,0:T(8,128)S(1)} %get-tuple-element.131), channel_id=1, source_target_pairs={{0,2},{1,3},{4,6},{5,7},{8,10},{9,11},{12,14},{13,15},{16,18},{17,... | collective-permute-start | bytes 196616 | tf_op jit(solution)/shard_map/ppermute | solution.py:22
  63.3 14.0 %all_gather.13 = f32[4,8,256]{2,0,1:T(4,128)S(1)} all-gather(f32[4,1,256]{2,0,1:T(4,128)S(1)} %slice.182), channel_id=1, replica_groups=mesh['groups'=2,'pipe'=4,'hour'=2,'seg'=2] {'pipe','seg'}, dimensions={1}, use_global_device_ids=true | all-gather | bytes 36864 | tf_op jit(solution)/shard_map/all_gather | solution.py:36
  78.7 2.2 collective-permute-start.6
  87.5 4.5 %collective-permute-start.8 = (f32[2,1,32,256]{3,2,1,0:T(8,128)S(1)}, f32[2,1,32,256]{3,2,1,0:T(8,128)S(1)}, u32[]{:S(2)}, u32[]{:S(2)}) collective-permute-start(f32[2,1,32,256]{3,2,1,0:T(8,128)S(1)} %get-tuple-element.127), channel_id=1, source_target_pairs={{0,2},{1,3},{4,6},{5,7},{8,10},{9,11},{12,14},{13,15},{16,18},{17,... | collective-permute-start | bytes 196616 | tf_op jit(solution)/shard_map/ppermute | solution.py:22
  92.0 4.5 %all-to-all-start.1 = ((f32[4,32,256]{2,0,1:T(4,128)}), f32[4,32,256]{2,0,1:T(4,128)S(1)}, u32[]{:S(2)}, u32[]{:S(2)}) async-start(f32[4,32,256]{2,0,1:T(4,128)} %multiply_subtract_fusion.3), calls=%async_computation.1 | async-start | bytes 262144 | tf_op jit(solution)/shard_map/all_to_all | solution.py:159
  98.5 14.6 %all_gather.14 = f32[4,8,256]{2,0,1:T(4,128)S(1)} all-gather(f32[4,1,256]{2,0,1:T(4,128)S(1)} %slice.191), channel_id=1, replica_groups=mesh['groups'=2,'pipe'=4,'hour'=2,'seg'=2] {'pipe','seg'}, dimensions={1}, use_global_device_ids=true | all-gather | bytes 36864 | tf_op jit(solution)/shard_map/all_gather | solution.py:36
  120.7 2.2 fusion.73
  125.6 3.1 %reshape.118 = f32[4,1,8192]{2,1,0:T(1,128)} reshape(f32[1024,4,8]{2,1,0:T(4,128)S(1)} %bitcast.197) | data formatting | bytes 262144
  128.7 4.5 %all-to-all-start.2 = ((f32[4,1,8192]{2,1,0:T(1,128)}), f32[4,1,8192]{2,1,0:T(1,128)S(1)}, u32[]{:S(2)}, u32[]{:S(2)}) async-start(f32[4,1,8192]{2,1,0:T(1,128)} %reshape.118), calls=%async_computation.2 | async-start | bytes 262144 | tf_op jit(solution)/shard_map/all_to_all | solution.py:141
  135.1 33.5 %all-reduce.1 = (f32[]{:T(128)}, f32[]{:T(128)}) all-reduce(f32[]{:T(128)S(6)} %add.153, f32[]{:T(128)S(6)} %add.155), channel_id=1, replica_groups=mesh['groups'=2,'pipe'=4,'hour'=2,'seg'=2] {'pipe','hour','seg'}, use_global_device_ids=true, to_apply=%region_5.7 | all-reduce | flops 2 | bytes 16 | tf_op jit(solution)/shard_map/psum | solution.py:171
  171.0 2.5 reshape.119
  181.3 4.5 %collective-permute-start.12 = (f32[2,1,32,256]{3,2,1,0:T(8,128)S(1)}, f32[2,1,32,256]{3,2,1,0:T(8,128)S(1)}, u32[]{:S(2)}, u32[]{:S(2)}) collective-permute-start(f32[2,1,32,256]{3,2,1,0:T(8,128)S(1)} %get-tuple-element.123), channel_id=1, source_target_pairs={{0,2},{1,3},{4,6},{5,7},{8,10},{9,11},{12,14},{13,15},{16,18},{17,... | collective-permute-start | bytes 196616 | tf_op jit(solution)/shard_map/ppermute | solution.py:22
  187.2 3.5 %all-to-all-start.3 = ((f32[4,32,256]{2,0,1:T(4,128)}), f32[4,32,256]{2,0,1:T(4,128)S(1)}, u32[]{:S(2)}, u32[]{:S(2)}) async-start(f32[4,32,256]{2,0,1:T(4,128)} %multiply_subtract_fusion.1), calls=%async_computation.3 | async-start | bytes 262144 | tf_op jit(solution)/shard_map/all_to_all | solution.py:159
  190.7 14.6 %all_gather.15 = f32[4,8,256]{2,0,1:T(4,128)S(1)} all-gather(f32[4,1,256]{2,0,1:T(4,128)S(1)} %slice.198), channel_id=1, replica_groups=mesh['groups'=2,'pipe'=4,'hour'=2,'seg'=2] {'pipe','seg'}, dimensions={1}, use_global_device_ids=true | all-gather | bytes 36864 | tf_op jit(solution)/shard_map/all_gather | solution.py:36
  209.4 3.0 %collective-permute-start.14 = (f32[2,6,1,256]{1,3,2,0:T(8,128)S(1)}, f32[2,6,1,256]{1,3,2,0:T(8,128)S(1)}, u32[]{:S(2)}, u32[]{:S(2)}) collective-permute-start(f32[2,6,1,256]{1,3,2,0:T(8,128)S(1)} %copy.201), channel_id=1, source_target_pairs={{0,1},{2,3},{4,5},{6,7},{8,9},{10,11},{12,13},{14,15},{16,17},{18,... | collective-permute-start | bytes 36872 | tf_op jit(solution)/shard_map/ppermute | solution.py:22
  217.6 2.4 multiply_reduce_fusion.8
  221.4 32.0 %all-reduce = (f32[]{:T(128)}, f32[]{:T(128)}) all-reduce(f32[]{:T(128)S(6)} %add.167, f32[]{:T(128)S(6)} %add.169), channel_id=1, replica_groups=mesh['groups'=2,'pipe'=4,'hour'=2,'seg'=2] {'pipe','hour','seg'}, use_global_device_ids=true, to_apply=%region_12.14 | all-reduce | flops 2 | bytes 16 | tf_op jit(solution)/shard_map/psum | solution.py:171
  (159 shorter events, 56.0 us)
Async XLA Ops:
  3.7 35.3 %copy-start.11 = (s32[32,256]{1,0:T(8,128)S(1)}, s32[32,256]{1,0:T(8,128)}, u32[]{:S(2)}) copy-start(s32[32,256]{1,0:T(8,128)} %param.23) | copy-start | bytes 98308
  3.7 35.3 %copy-start.13 = (f32[16]{0:T(128)S(1)}, f32[16]{0:T(128)}, u32[]{:S(2)}) copy-start(f32[16]{0:T(128)} %param.22) | copy-start | bytes 196
  6.8 39.5 %all-to-all-start = ((f32[4,1,8192]{2,1,0:T(1,128)}), f32[4,1,8192]{2,1,0:T(1,128)S(1)}, u32[]{:S(2)}, u32[]{:S(2)}) async-start(f32[4,1,8192]{2,1,0:T(1,128)} %reshape.116), calls=%async_computation | async-start | bytes 262144 | tf_op jit(solution)/shard_map/all_to_all | solution.py:141
  13.2 26.8 %collective-permute-start.1 = (f32[2,1,32,256]{3,2,1,0:T(8,128)S(1)}, f32[2,1,32,256]{3,2,1,0:T(8,128)S(1)}, u32[]{:S(2)}, u32[]{:S(2)}) collective-permute-start(f32[2,1,32,256]{3,2,1,0:T(8,128)S(1)} %get-tuple-element.136), channel_id=1, source_target_pairs={{2,0},{3,1},{6,4},{7,5},{10,8},{11,9},{14,12},{15,13},{18,16},{19,... | collective-permute-start | bytes 196616 | tf_op jit(solution)/shard_map/ppermute | solution.py:24
  14.5 25.5 %collective-permute-start = (f32[2,1,32,256]{3,2,1,0:T(8,128)S(1)}, f32[2,1,32,256]{3,2,1,0:T(8,128)S(1)}, u32[]{:S(2)}, u32[]{:S(2)}) collective-permute-start(f32[2,1,32,256]{3,2,1,0:T(8,128)S(1)} %get-tuple-element.135), channel_id=1, source_target_pairs={{0,2},{1,3},{4,6},{5,7},{8,10},{9,11},{12,14},{13,15},{16,18},{17,... | collective-permute-start | bytes 196616 | tf_op jit(solution)/shard_map/ppermute | solution.py:22
  40.3 13.8 %collective-permute-start.3 = (f32[2,6,1,256]{3,1,2,0:T(8,128)S(1)}, f32[2,6,1,256]{3,1,2,0:T(8,128)S(1)}, u32[]{:S(2)}, u32[]{:S(2)}) collective-permute-start(f32[2,6,1,256]{3,1,2,0:T(8,128)S(1)} %slice.177), channel_id=1, source_target_pairs={{0,1},{2,3},{4,5},{6,7},{8,9},{10,11},{12,13},{14,15},{16,17},{18,... | collective-permute-start | bytes 36872 | tf_op jit(solution)/shard_map/ppermute | solution.py:22
  42.7 3.4 %collective-permute-start.2 = (f32[2,6,1,256]{1,3,2,0:T(8,128)S(1)}, f32[2,6,1,256]{1,3,2,0:T(8,128)S(1)}, u32[]{:S(2)}, u32[]{:S(2)}) collective-permute-start(f32[2,6,1,256]{1,3,2,0:T(8,128)S(1)} %copy.191), channel_id=1, source_target_pairs={{1,0},{3,2},{5,4},{7,6},{9,8},{11,10},{13,12},{15,14},{17,16},{19,... | collective-permute-start | bytes 36872 | tf_op jit(solution)/shard_map/ppermute | solution.py:24
  57.2 21.0 %collective-permute-start.5 = (f32[2,1,32,256]{3,2,1,0:T(8,128)S(1)}, f32[2,1,32,256]{3,2,1,0:T(8,128)S(1)}, u32[]{:S(2)}, u32[]{:S(2)}) collective-permute-start(f32[2,1,32,256]{3,2,1,0:T(8,128)S(1)} %get-tuple-element.132), channel_id=1, source_target_pairs={{2,0},{3,1},{6,4},{7,5},{10,8},{11,9},{14,12},{15,13},{18,16},{19,... | collective-permute-start | bytes 196616 | tf_op jit(solution)/shard_map/ppermute | solution.py:24
  58.7 19.6 %collective-permute-start.4 = (f32[2,1,32,256]{3,2,1,0:T(8,128)S(1)}, f32[2,1,32,256]{3,2,1,0:T(8,128)S(1)}, u32[]{:S(2)}, u32[]{:S(2)}) collective-permute-start(f32[2,1,32,256]{3,2,1,0:T(8,128)S(1)} %get-tuple-element.131), channel_id=1, source_target_pairs={{0,2},{1,3},{4,6},{5,7},{8,10},{9,11},{12,14},{13,15},{16,18},{17,... | collective-permute-start | bytes 196616 | tf_op jit(solution)/shard_map/ppermute | solution.py:22
  78.7 3.7 %collective-permute-start.6 = (f32[2,6,1,256]{1,3,2,0:T(8,128)S(1)}, f32[2,6,1,256]{1,3,2,0:T(8,128)S(1)}, u32[]{:S(2)}, u32[]{:S(2)}) collective-permute-start(f32[2,6,1,256]{1,3,2,0:T(8,128)S(1)} %copy.195), channel_id=1, source_target_pairs={{0,1},{2,3},{4,5},{6,7},{8,9},{10,11},{12,13},{14,15},{16,17},{18,... | collective-permute-start | bytes 36872 | tf_op jit(solution)/shard_map/ppermute | solution.py:22
  81.0 3.1 %collective-permute-start.7 = (f32[2,6,1,256]{3,1,2,0:T(8,128)S(1)}, f32[2,6,1,256]{3,1,2,0:T(8,128)S(1)}, u32[]{:S(2)}, u32[]{:S(2)}) collective-permute-start(f32[2,6,1,256]{3,1,2,0:T(8,128)S(1)} %slice.185), channel_id=1, source_target_pairs={{1,0},{3,2},{5,4},{7,6},{9,8},{11,10},{13,12},{15,14},{17,16},{19,... | collective-permute-start | bytes 36872 | tf_op jit(solution)/shard_map/ppermute | solution.py:24
  86.1 34.6 %copy-start.14 = (f32[4,1,8,128]{3,2,1,0:T(8,128)S(1)}, f32[4,1,8,128]{3,2,1,0:T(8,128)}, u32[]{:S(2)}) copy-start(f32[4,1,8,128]{3,2,1,0:T(8,128)} %param.18) | copy-start | bytes 49156
  86.1 34.6 %copy-start.15 = (s32[4,1024]{1,0:T(4,128)S(1)}, s32[4,1024]{1,0:T(4,128)}, u32[]{:S(2)}) copy-start(s32[4,1024]{1,0:T(4,128)} %param.25) | copy-start | bytes 49156
  86.2 29.8 %collective-permute-start.9 = (f32[2,1,32,256]{3,2,1,0:T(8,128)S(1)}, f32[2,1,32,256]{3,2,1,0:T(8,128)S(1)}, u32[]{:S(2)}, u32[]{:S(2)}) collective-permute-start(f32[2,1,32,256]{3,2,1,0:T(8,128)S(1)} %get-tuple-element.128), channel_id=1, source_target_pairs={{2,0},{3,1},{6,4},{7,5},{10,8},{11,9},{14,12},{15,13},{18,16},{19,... | collective-permute-start | bytes 196616 | tf_op jit(solution)/shard_map/ppermute | solution.py:24
  87.5 28.5 %collective-permute-start.8 = (f32[2,1,32,256]{3,2,1,0:T(8,128)S(1)}, f32[2,1,32,256]{3,2,1,0:T(8,128)S(1)}, u32[]{:S(2)}, u32[]{:S(2)}) collective-permute-start(f32[2,1,32,256]{3,2,1,0:T(8,128)S(1)} %get-tuple-element.127), channel_id=1, source_target_pairs={{0,2},{1,3},{4,6},{5,7},{8,10},{9,11},{12,14},{13,15},{16,18},{17,... | collective-permute-start | bytes 196616 | tf_op jit(solution)/shard_map/ppermute | solution.py:22
  92.0 28.6 %all-to-all-start.1 = ((f32[4,32,256]{2,0,1:T(4,128)}), f32[4,32,256]{2,0,1:T(4,128)S(1)}, u32[]{:S(2)}, u32[]{:S(2)}) async-start(f32[4,32,256]{2,0,1:T(4,128)} %multiply_subtract_fusion.3), calls=%async_computation.1 | async-start | bytes 262144 | tf_op jit(solution)/shard_map/all_to_all | solution.py:159
  116.3 61.0 %collective-permute-start.11 = (f32[2,6,1,256]{3,1,2,0:T(8,128)S(1)}, f32[2,6,1,256]{3,1,2,0:T(8,128)S(1)}, u32[]{:S(2)}, u32[]{:S(2)}) collective-permute-start(f32[2,6,1,256]{3,1,2,0:T(8,128)S(1)} %slice.193), channel_id=1, source_target_pairs={{0,1},{2,3},{4,5},{6,7},{8,9},{10,11},{12,13},{14,15},{16,17},{18,... | collective-permute-start | bytes 36872 | tf_op jit(solution)/shard_map/ppermute | solution.py:22
  119.3 13.9 %collective-permute-start.10 = (f32[2,6,1,256]{1,3,2,0:T(8,128)}, f32[2,6,1,256]{1,3,2,0:T(8,128)}, u32[]{:S(2)}, u32[]{:S(2)}) collective-permute-start(f32[2,6,1,256]{1,3,2,0:T(8,128)} %copy.197), channel_id=1, source_target_pairs={{1,0},{3,2},{5,4},{7,6},{9,8},{11,10},{13,12},{15,14},{17,16},{19,... | collective-permute-start | bytes 36872 | tf_op jit(solution)/shard_map/ppermute | solution.py:24
  128.7 41.3 %all-to-all-start.2 = ((f32[4,1,8192]{2,1,0:T(1,128)}), f32[4,1,8192]{2,1,0:T(1,128)S(1)}, u32[]{:S(2)}, u32[]{:S(2)}) async-start(f32[4,1,8192]{2,1,0:T(1,128)} %reshape.118), calls=%async_computation.2 | async-start | bytes 262144 | tf_op jit(solution)/shard_map/all_to_all | solution.py:141
  180.0 27.6 %collective-permute-start.13 = (f32[2,1,32,256]{3,2,1,0:T(8,128)S(1)}, f32[2,1,32,256]{3,2,1,0:T(8,128)S(1)}, u32[]{:S(2)}, u32[]{:S(2)}) collective-permute-start(f32[2,1,32,256]{3,2,1,0:T(8,128)S(1)} %get-tuple-element.124), channel_id=1, source_target_pairs={{2,0},{3,1},{6,4},{7,5},{10,8},{11,9},{14,12},{15,13},{18,16},{19,... | collective-permute-start | bytes 196616 | tf_op jit(solution)/shard_map/ppermute | solution.py:24
  181.3 26.3 %collective-permute-start.12 = (f32[2,1,32,256]{3,2,1,0:T(8,128)S(1)}, f32[2,1,32,256]{3,2,1,0:T(8,128)S(1)}, u32[]{:S(2)}, u32[]{:S(2)}) collective-permute-start(f32[2,1,32,256]{3,2,1,0:T(8,128)S(1)} %get-tuple-element.123), channel_id=1, source_target_pairs={{0,2},{1,3},{4,6},{5,7},{8,10},{9,11},{12,14},{13,15},{16,18},{17,... | collective-permute-start | bytes 196616 | tf_op jit(solution)/shard_map/ppermute | solution.py:22
  187.2 30.4 %all-to-all-start.3 = ((f32[4,32,256]{2,0,1:T(4,128)}), f32[4,32,256]{2,0,1:T(4,128)S(1)}, u32[]{:S(2)}, u32[]{:S(2)}) async-start(f32[4,32,256]{2,0,1:T(4,128)} %multiply_subtract_fusion.1), calls=%async_computation.3 | async-start | bytes 262144 | tf_op jit(solution)/shard_map/all_to_all | solution.py:159
  207.9 5.8 %collective-permute-start.15 = (f32[2,6,1,256]{3,1,2,0:T(8,128)S(1)}, f32[2,6,1,256]{3,1,2,0:T(8,128)S(1)}, u32[]{:S(2)}, u32[]{:S(2)}) collective-permute-start(f32[2,6,1,256]{3,1,2,0:T(8,128)S(1)} %slice.201), channel_id=1, source_target_pairs={{1,0},{3,2},{5,4},{7,6},{9,8},{11,10},{13,12},{15,14},{17,16},{19,... | collective-permute-start | bytes 36872 | tf_op jit(solution)/shard_map/ppermute | solution.py:24
  209.4 4.2 %collective-permute-start.14 = (f32[2,6,1,256]{1,3,2,0:T(8,128)S(1)}, f32[2,6,1,256]{1,3,2,0:T(8,128)S(1)}, u32[]{:S(2)}, u32[]{:S(2)}) collective-permute-start(f32[2,6,1,256]{1,3,2,0:T(8,128)S(1)} %copy.201), channel_id=1, source_target_pairs={{0,1},{2,3},{4,5},{6,7},{8,9},{10,11},{12,13},{14,15},{16,17},{18,... | collective-permute-start | bytes 36872 | tf_op jit(solution)/shard_map/ppermute | solution.py:22
  (13 other events, 152.4 us)
where the time goes:
time: 257 us; the launch traced here: 256 us
  blocking collectives  123 us (48%)
  starting transfers between devices  57.3 us (22%)
  local copies, waits for them, and re-layouts  34.9 us (14%)
  other arithmetic  15.8 us (6%)
  between operations  12.1 us (5%)
  matrix products  8.66 us (3%)
  waiting for transfers between devices  3.97 us (2%)
    psum x2, blocking collectives, on_device(): lax.psum((primal_sq, dual_sq), ('pipe', 'hour', 'seg'))  65.5 us
    all_gather x4, blocking collectives, other_half(): lax.all_gather(edge_row[:, None, :], ('pipe', 'seg'), axis=1, tiled=True)  57.8 us
    ppermute x8, starting transfers between devices, padded(): lax.ppermute(tail, axis, [(i, (i + 1) % count) for i in range(ends)])  27.9 us
    unnamed x55, local copies, waits for them, and re-layouts  17 us
    all_to_all x2, starting transfers between devices, on_device(): lax.all_to_all(hour_spread, 'pipe', split_axis=2, concat_axis=1, tiled=True)  10.8 us
    ppermute x8, starting transfers between devices, padded(): lax.ppermute(head, axis, [((i + 1) % count, i) for i in range(ends)])  10.6 us
    all_to_all x2, starting transfers between devices, on_device(): lax.all_to_all(pack_bar, 'pipe', split_axis=1, concat_axis=2, tiled=True)  7.96 us
  transfers between devices with their start and end apart: 20, of which 3 were waited for; matrix products, arithmetic and copies ran while one was open for 16% of the time, Pallas kernels for 0%

commit v1 on v0

--- a/solution.py
+++ b/solution.py
@@ -3,6 +3,7 @@
 import jax.numpy as jnp
 from jax import lax
 from jax.sharding import PartitionSpec as P
+from jax.lax import axis_index, axis_size, ppermute
 
 ITERS = 2
 FLOW_CAP = 1.5
@@ -33,7 +34,29 @@
 
 
 def other_half(edge_row, half_index, partner_local):
-    gathered = lax.all_gather(edge_row[:, None, :], ("pipe", "seg"), axis=1, tiled=True)
+
+    def _produce_state(own_rows, axis_key, where_dim):
+        latest, d_next, block_last = (
+            axis_size(axis_key),
+            axis_index(axis_key),
+            own_rows.shape[where_dim],
+        )
+        by_rank = list(map(lambda u: (u, (u + 1) % latest), range(latest)))
+        passed = own_rows
+        block_now = jnp.zeros(
+            (*own_rows.shape[:where_dim], latest * block_last, *own_rows.shape[where_dim + 1 :]),
+            own_rows.dtype,
+        )
+        for src_i in range(latest):
+            w2 = (d_next - src_i) % latest
+            block_now = lax.dynamic_update_slice_in_dim(
+                block_now, passed, w2 * block_last, axis=where_dim
+            )
+            if src_i < latest - 1:
+                passed = ppermute(passed, axis_key, by_rank)
+        return block_now
+
+    gathered = _produce_state(edge_row[:, None, :], ("pipe", "seg"), 1)
     hour_rows, row_count, row_width = gathered.shape
     seg_count = lax.axis_size("seg")
     picked = gathered.reshape(hour_rows, row_count // seg_count, seg_count, row_width)[

time: 257 us -> 313 us (1.22)
  waiting for transfers between devices: 3.97 us -> 116 us
  blocking collectives: 123 us -> 64.1 us
    ppermute x0 -> x28, waiting for transfers between devices: none -> 112 us  [_produce_state(): passed = ppermute(passed, axis_key, by_rank)]
    all_gather x4 -> x0, blocking collectives: 57.8 us -> none  [other_half(): lax.all_gather(edge_row[:, None, :], ('pipe', 'seg'), axis=1, tiled=True)]
    ppermute x0 -> x28, starting transfers between devices: none -> 5.19 us  [_produce_state(): passed = ppermute(passed, axis_key, by_rank)]
    unnamed x55 -> x48, local copies, waits for them, and re-layouts: 17 us -> 17 us
  transfers between devices with their start and end apart: 20 -> 48, of which waited for: 3 -> 27; matrix products, arithmetic and copies ran while one was open for 16% -> 15% of each run, Pallas kernels for 0% -> 0%
where the time goes in v1:
time: 313 us; the launch traced here: 312 us
  waiting for transfers between devices  116 us (37%)
  blocking collectives  64.1 us (20%)
  starting transfers between devices  57.2 us (18%)
  local copies, waits for them, and re-layouts  36.9 us (12%)
  other arithmetic  16.4 us (5%)
  between operations  12.2 us (4%)
  matrix products  8.93 us (3%)
    ppermute x28, waiting for transfers between devices, _produce_state(): passed = ppermute(passed, axis_key, by_rank)  112 us
    psum x2, blocking collectives, on_device(): lax.psum((primal_sq, dual_sq), ('pipe', 'hour', 'seg'))  64.1 us
    ppermute x8, starting transfers between devices, padded(): lax.ppermute(tail, axis, [(i, (i + 1) % count) for i in range(ends)])  25.3 us
    unnamed x48, local copies, waits for them, and re-layouts  17 us
    ppermute x8, starting transfers between devices, padded(): lax.ppermute(head, axis, [((i + 1) % count, i) for i in range(ends)])  10.4 us
    all_to_all x2, starting transfers between devices, on_device(): lax.all_to_all(hour_spread, 'pipe', split_axis=2, concat_axis=1, tiled=True)  9.64 us
    all_to_all x2, starting transfers between devices, on_device(): lax.all_to_all(pack_bar, 'pipe', split_axis=1, concat_axis=2, tiled=True)  6.66 us
  transfers between devices with their start and end apart: 48, of which 27 were waited for; matrix products, arithmetic and copies ran while one was open for 15% of the time, Pallas kernels for 0%

profile of v1, /device:TPU:0, one launch (start us, length us, event | category | flops | bytes accessed | tf_op | source)
XLA Modules:
  0.0 311.7 jit_solution(13467952064483631409)
XLA Ops:
  6.8 6.3 %all-to-all-start = ((f32[4,1,8192]{2,1,0:T(1,128)}), f32[4,1,8192]{2,1,0:T(1,128)S(1)}, u32[]{:S(2)}, u32[]{:S(2)}) async-start(f32[4,1,8192]{2,1,0:T(1,128)} %reshape.116), calls=%async_computation | async-start | bytes 262144 | tf_op jit(solution)/shard_map/all_to_all | solution.py:164
  29.6 4.8 %collective-permute-done.5 = f32[4,1,256]{2,1,0:T(1,128)S(1)} collective-permute-done((f32[4,1,256]{2,1,0:T(1,128)S(1)}, f32[4,1,256]{2,1,0:T(1,128)S(1)}, u32[]{:S(2)}, u32[]{:S(2)}) %collective-permute-start.5) | collective-permute-done | bytes 4128 | tf_op jit(solution)/shard_map/ppermute | solution.py:56
  34.4 4.8 %collective-permute-done.6 = f32[4,1,256]{2,1,0:T(1,128)S(1)} collective-permute-done((f32[4,1,256]{2,1,0:T(1,128)S(1)}, f32[4,1,256]{2,1,0:T(1,128)S(1)}, u32[]{:S(2)}, u32[]{:S(2)}) %collective-permute-start.6) | collective-permute-done | bytes 4128 | tf_op jit(solution)/shard_map/ppermute | solution.py:56
  39.2 4.8 %collective-permute-done.7 = f32[4,1,256]{2,1,0:T(1,128)S(1)} collective-permute-done((f32[4,1,256]{2,1,0:T(1,128)S(1)}, f32[4,1,256]{2,1,0:T(1,128)S(1)}, u32[]{:S(2)}, u32[]{:S(2)}) %collective-permute-start.7) | collective-permute-done | bytes 4128 | tf_op jit(solution)/shard_map/ppermute | solution.py:56
  44.1 4.8 %collective-permute-done.8 = f32[4,1,256]{2,1,0:T(1,128)S(1)} collective-permute-done((f32[4,1,256]{2,1,0:T(1,128)S(1)}, f32[4,1,256]{2,1,0:T(1,128)S(1)}, u32[]{:S(2)}, u32[]{:S(2)}) %collective-permute-start.8) | collective-permute-done | bytes 4128 | tf_op jit(solution)/shard_map/ppermute | solution.py:56
  48.9 4.8 %collective-permute-done.9 = f32[4,1,256]{2,1,0:T(1,128)S(1)} collective-permute-done((f32[4,1,256]{2,1,0:T(1,128)S(1)}, f32[4,1,256]{2,1,0:T(1,128)S(1)}, u32[]{:S(2)}, u32[]{:S(2)}) %collective-permute-start.9) | collective-permute-done | bytes 4128 | tf_op jit(solution)/shard_map/ppermute | solution.py:56
  86.8 4.8 %collective-permute-done.16 = f32[4,1,256]{2,0,1:T(4,128)S(1)} collective-permute-done((f32[4,1,256]{2,0,1:T(4,128)S(1)}, f32[4,1,256]{2,0,1:T(4,128)S(1)}, u32[]{:S(2)}, u32[]{:S(2)}) %collective-permute-start.16) | collective-permute-done | bytes 4128 | tf_op jit(solution)/shard_map/ppermute | solution.py:56
  91.6 4.8 %collective-permute-done.17 = f32[4,1,256]{2,0,1:T(4,128)S(1)} collective-permute-done((f32[4,1,256]{2,0,1:T(4,128)S(1)}, f32[4,1,256]{2,0,1:T(4,128)S(1)}, u32[]{:S(2)}, u32[]{:S(2)}) %collective-permute-start.17) | collective-permute-done | bytes 4128 | tf_op jit(solution)/shard_map/ppermute | solution.py:56
  96.5 4.8 %collective-permute-done.18 = f32[4,1,256]{2,0,1:T(4,128)S(1)} collective-permute-done((f32[4,1,256]{2,0,1:T(4,128)S(1)}, f32[4,1,256]{2,0,1:T(4,128)S(1)}, u32[]{:S(2)}, u32[]{:S(2)}) %collective-permute-start.18) | collective-permute-done | bytes 4128 | tf_op jit(solution)/shard_map/ppermute | solution.py:56
  101.3 4.8 %collective-permute-done.19 = f32[4,1,256]{2,0,1:T(4,128)S(1)} collective-permute-done((f32[4,1,256]{2,0,1:T(4,128)S(1)}, f32[4,1,256]{2,0,1:T(4,128)S(1)}, u32[]{:S(2)}, u32[]{:S(2)}) %collective-permute-start.19) | collective-permute-done | bytes 4128 | tf_op jit(solution)/shard_map/ppermute | solution.py:56
  106.1 4.8 %collective-permute-done.20 = f32[4,1,256]{2,0,1:T(4,128)S(1)} collective-permute-done((f32[4,1,256]{2,0,1:T(4,128)S(1)}, f32[4,1,256]{2,0,1:T(4,128)S(1)}, u32[]{:S(2)}, u32[]{:S(2)}) %collective-permute-start.20) | collective-permute-done | bytes 4128 | tf_op jit(solution)/shard_map/ppermute | solution.py:56
  127.2 4.8 %collective-permute-done.26 = f32[4,1,256]{2,0,1:T(4,128)S(1)} collective-permute-done((f32[4,1,256]{2,0,1:T(4,128)S(1)}, f32[4,1,256]{2,0,1:T(4,128)S(1)}, u32[]{:S(2)}, u32[]{:S(2)}) %collective-permute-start.26) | collective-permute-done | bytes 4128 | tf_op jit(solution)/shard_map/ppermute | solution.py:56
  132.0 4.8 %collective-permute-done.27 = f32[4,1,256]{2,0,1:T(4,128)S(1)} collective-permute-done((f32[4,1,256]{2,0,1:T(4,128)S(1)}, f32[4,1,256]{2,0,1:T(4,128)S(1)}, u32[]{:S(2)}, u32[]{:S(2)}) %collective-permute-start.27) | collective-permute-done | bytes 4128 | tf_op jit(solution)/shard_map/ppermute | solution.py:56
  136.8 4.8 %collective-permute-done.28 = f32[4,1,256]{2,0,1:T(4,128)S(1)} collective-permute-done((f32[4,1,256]{2,0,1:T(4,128)S(1)}, f32[4,1,256]{2,0,1:T(4,128)S(1)}, u32[]{:S(2)}, u32[]{:S(2)}) %collective-permute-start.28) | collective-permute-done | bytes 4128 | tf_op jit(solution)/shard_map/ppermute | solution.py:56
  141.6 4.8 %collective-permute-done.29 = f32[4,1,256]{2,0,1:T(4,128)S(1)} collective-permute-done((f32[4,1,256]{2,0,1:T(4,128)S(1)}, f32[4,1,256]{2,0,1:T(4,128)S(1)}, u32[]{:S(2)}, u32[]{:S(2)}) %collective-permute-start.29) | collective-permute-done | bytes 4128 | tf_op jit(solution)/shard_map/ppermute | solution.py:56
  146.5 4.8 %collective-permute-done.30 = f32[4,1,256]{2,0,1:T(4,128)S(1)} collective-permute-done((f32[4,1,256]{2,0,1:T(4,128)S(1)}, f32[4,1,256]{2,0,1:T(4,128)S(1)}, u32[]{:S(2)}, u32[]{:S(2)}) %collective-permute-start.30) | collective-permute-done | bytes 4128 | tf_op jit(solution)/shard_map/ppermute | solution.py:56
  151.3 4.8 %collective-permute-done.31 = f32[4,1,256]{2,0,1:T(4,128)S(1)} collective-permute-done((f32[4,1,256]{2,0,1:T(4,128)S(1)}, f32[4,1,256]{2,0,1:T(4,128)S(1)}, u32[]{:S(2)}, u32[]{:S(2)}) %collective-permute-start.31) | collective-permute-done | bytes 4128 | tf_op jit(solution)/shard_map/ppermute | solution.py:56
  175.8 33.7 %all-reduce.1 = (f32[]{:T(128)}, f32[]{:T(128)}) all-reduce(f32[]{:T(128)S(6)} %add.280, f32[]{:T(128)S(6)} %add.282), channel_id=1, replica_groups=mesh['groups'=2,'pipe'=4,'hour'=2,'seg'=2] {'pipe','hour','seg'}, use_global_device_ids=true, to_apply=%region_5.7 | all-reduce | flops 2 | bytes 16 | tf_op jit(solution)/shard_map/psum | solution.py:194
  240.0 4.8 %collective-permute-done.38 = f32[4,1,256]{2,0,1:T(4,128)S(1)} collective-permute-done((f32[4,1,256]{2,0,1:T(4,128)S(1)}, f32[4,1,256]{2,0,1:T(4,128)S(1)}, u32[]{:S(2)}, u32[]{:S(2)}) %collective-permute-start.38) | collective-permute-done | bytes 4128 | tf_op jit(solution)/shard_map/ppermute | solution.py:56
  244.8 4.8 %collective-permute-done.39 = f32[4,1,256]{2,0,1:T(4,128)S(1)} collective-permute-done((f32[4,1,256]{2,0,1:T(4,128)S(1)}, f32[4,1,256]{2,0,1:T(4,128)S(1)}, u32[]{:S(2)}, u32[]{:S(2)}) %collective-permute-start.39) | collective-permute-done | bytes 4128 | tf_op jit(solution)/shard_map/ppermute | solution.py:56
  249.7 4.8 %collective-permute-done.40 = f32[4,1,256]{2,0,1:T(4,128)S(1)} collective-permute-done((f32[4,1,256]{2,0,1:T(4,128)S(1)}, f32[4,1,256]{2,0,1:T(4,128)S(1)}, u32[]{:S(2)}, u32[]{:S(2)}) %collective-permute-start.40) | collective-permute-done | bytes 4128 | tf_op jit(solution)/shard_map/ppermute | solution.py:56
  254.5 4.8 %collective-permute-done.41 = f32[4,1,256]{2,0,1:T(4,128)S(1)} collective-permute-done((f32[4,1,256]{2,0,1:T(4,128)S(1)}, f32[4,1,256]{2,0,1:T(4,128)S(1)}, u32[]{:S(2)}, u32[]{:S(2)}) %collective-permute-start.41) | collective-permute-done | bytes 4128 | tf_op jit(solution)/shard_map/ppermute | solution.py:56
  259.3 4.8 %collective-permute-done.42 = f32[4,1,256]{2,0,1:T(4,128)S(1)} collective-permute-done((f32[4,1,256]{2,0,1:T(4,128)S(1)}, f32[4,1,256]{2,0,1:T(4,128)S(1)}, u32[]{:S(2)}, u32[]{:S(2)}) %collective-permute-start.42) | collective-permute-done | bytes 4128 | tf_op jit(solution)/shard_map/ppermute | solution.py:56
  278.9 30.3 %all-reduce = (f32[]{:T(128)}, f32[]{:T(128)}) all-reduce(f32[]{:T(128)S(6)} %add.294, f32[]{:T(128)S(6)} %add.296), channel_id=1, replica_groups=mesh['groups'=2,'pipe'=4,'hour'=2,'seg'=2] {'pipe','hour','seg'}, use_global_device_ids=true, to_apply=%region_12.14 | all-reduce | flops 2 | bytes 16 | tf_op jit(solution)/shard_map/psum | solution.py:194
  (241 shorter events, 128.0 us)
Async XLA Ops:
  6.8 53.3 %all-to-all-start = ((f32[4,1,8192]{2,1,0:T(1,128)}), f32[4,1,8192]{2,1,0:T(1,128)S(1)}, u32[]{:S(2)}, u32[]{:S(2)}) async-start(f32[4,1,8192]{2,1,0:T(1,128)} %reshape.116), calls=%async_computation | async-start | bytes 262144 | tf_op jit(solution)/shard_map/all_to_all | solution.py:164
  13.2 41.5 %collective-permute-start.1 = (f32[2,1,32,256]{3,2,1,0:T(8,128)S(1)}, f32[2,1,32,256]{3,2,1,0:T(8,128)S(1)}, u32[]{:S(2)}, u32[]{:S(2)}) collective-permute-start(f32[2,1,32,256]{3,2,1,0:T(8,128)S(1)} %get-tuple-element.142), channel_id=1, source_target_pairs={{2,0},{3,1},{6,4},{7,5},{10,8},{11,9},{14,12},{15,13},{18,16},{19,... | collective-permute-start | bytes 196616 | tf_op jit(solution)/shard_map/ppermute | solution.py:25
  14.5 40.2 %collective-permute-start = (f32[2,1,32,256]{3,2,1,0:T(8,128)S(1)}, f32[2,1,32,256]{3,2,1,0:T(8,128)S(1)}, u32[]{:S(2)}, u32[]{:S(2)}) collective-permute-start(f32[2,1,32,256]{3,2,1,0:T(8,128)S(1)} %get-tuple-element.141), channel_id=1, source_target_pairs={{0,2},{1,3},{4,6},{5,7},{8,10},{9,11},{12,14},{13,15},{16,18},{17,... | collective-permute-start | bytes 196616 | tf_op jit(solution)/shard_map/ppermute | solution.py:23
  19.0 5.7 %collective-permute-start.3 = (f32[4,1,256]{2,1,0:T(1,128)S(1)}, f32[4,1,256]{2,1,0:T(1,128)S(1)}, u32[]{:S(2)}, u32[]{:S(2)}) collective-permute-start(f32[4,1,256]{2,1,0:T(1,128)S(1)} %slice.129), channel_id=1, source_target_pairs={{0,1},{1,4},{4,5},{5,8},{8,9},{9,12},{12,13},{13,0},{2,3},{3,6},{6... | collective-permute-start | bytes 12296 | tf_op jit(solution)/shard_map/ppermute | solution.py:56
  24.7 4.8 %collective-permute-start.4 = (f32[4,1,256]{2,1,0:T(1,128)S(1)}, f32[4,1,256]{2,1,0:T(1,128)S(1)}, u32[]{:S(2)}, u32[]{:S(2)}) collective-permute-start(f32[4,1,256]{2,1,0:T(1,128)S(1)} %collective-permute-done.3), channel_id=1, source_target_pairs={{0,1},{1,4},{4,5},{5,8},{8,9},{9,12},{12,13},{13,0},{2,3},{3,6},{6... | collective-permute-start | bytes 12296 | tf_op jit(solution)/shard_map/ppermute | solution.py:56
  55.0 12.9 %collective-permute-start.10 = (f32[2,6,1,256]{3,1,2,0:T(8,128)S(1)}, f32[2,6,1,256]{3,1,2,0:T(8,128)S(1)}, u32[]{:S(2)}, u32[]{:S(2)}) collective-permute-start(f32[2,6,1,256]{3,1,2,0:T(8,128)S(1)} %slice.176), channel_id=1, source_target_pairs={{0,1},{2,3},{4,5},{6,7},{8,9},{10,11},{12,13},{14,15},{16,17},{18,... | collective-permute-start | bytes 36872 | tf_op jit(solution)/shard_map/ppermute | solution.py:23
  69.9 91.5 %all-to-all-start.1 = ((f32[4,32,256]{2,0,1:T(4,128)}), f32[4,32,256]{2,0,1:T(4,128)S(1)}, u32[]{:S(2)}, u32[]{:S(2)}) async-start(f32[4,32,256]{2,0,1:T(4,128)} %multiply_subtract_fusion.3), calls=%async_computation.1 | async-start | bytes 262144 | tf_op jit(solution)/shard_map/all_to_all | solution.py:182
  73.5 8.5 %collective-permute-start.14 = (f32[4,1,256]{2,0,1:T(4,128)S(1)}, f32[4,1,256]{2,0,1:T(4,128)S(1)}, u32[]{:S(2)}, u32[]{:S(2)}) collective-permute-start(f32[4,1,256]{2,0,1:T(4,128)S(1)} %get-tuple-element.147), channel_id=1, source_target_pairs={{0,1},{1,4},{4,5},{5,8},{8,9},{9,12},{12,13},{13,0},{2,3},{3,6},{6... | collective-permute-start | bytes 12296 | tf_op jit(solution)/shard_map/ppermute | solution.py:56
  74.6 37.3 %collective-permute-start.12 = (f32[2,1,32,256]{3,2,1,0:T(8,128)S(1)}, f32[2,1,32,256]{3,2,1,0:T(8,128)S(1)}, u32[]{:S(2)}, u32[]{:S(2)}) collective-permute-start(f32[2,1,32,256]{3,2,1,0:T(8,128)S(1)} %get-tuple-element.138), channel_id=1, source_target_pairs={{2,0},{3,1},{6,4},{7,5},{10,8},{11,9},{14,12},{15,13},{18,16},{19,... | collective-permute-start | bytes 196616 | tf_op jit(solution)/shard_map/ppermute | solution.py:25
  76.0 35.9 %collective-permute-start.11 = (f32[2,1,32,256]{3,2,1,0:T(8,128)S(1)}, f32[2,1,32,256]{3,2,1,0:T(8,128)S(1)}, u32[]{:S(2)}, u32[]{:S(2)}) collective-permute-start(f32[2,1,32,256]{3,2,1,0:T(8,128)S(1)} %get-tuple-element.137), channel_id=1, source_target_pairs={{0,2},{1,3},{4,6},{5,7},{8,10},{9,11},{12,14},{13,15},{16,18},{17,... | collective-permute-start | bytes 196616 | tf_op jit(solution)/shard_map/ppermute | solution.py:23
  81.9 4.9 %collective-permute-start.15 = (f32[4,1,256]{2,0,1:T(4,128)S(1)}, f32[4,1,256]{2,0,1:T(4,128)S(1)}, u32[]{:S(2)}, u32[]{:S(2)}) collective-permute-start(f32[4,1,256]{2,0,1:T(4,128)S(1)} %collective-permute-done.14), channel_id=1, source_target_pairs={{0,1},{1,4},{4,5},{5,8},{8,9},{9,12},{12,13},{13,0},{2,3},{3,6},{6... | collective-permute-start | bytes 12296 | tf_op jit(solution)/shard_map/ppermute | solution.py:56
  119.0 8.1 %collective-permute-start.25 = (f32[4,1,256]{2,0,1:T(4,128)S(1)}, f32[4,1,256]{2,0,1:T(4,128)S(1)}, u32[]{:S(2)}, u32[]{:S(2)}) collective-permute-start(f32[4,1,256]{2,0,1:T(4,128)S(1)} %get-tuple-element.145), channel_id=1, source_target_pairs={{0,1},{1,4},{4,5},{5,8},{8,9},{9,12},{12,13},{13,0},{2,3},{3,6},{6... | collective-permute-start | bytes 12296 | tf_op jit(solution)/shard_map/ppermute | solution.py:56
  119.9 37.8 %collective-permute-start.23 = (f32[2,1,32,256]{3,2,1,0:T(8,128)S(1)}, f32[2,1,32,256]{3,2,1,0:T(8,128)S(1)}, u32[]{:S(2)}, u32[]{:S(2)}) collective-permute-start(f32[2,1,32,256]{3,2,1,0:T(8,128)S(1)} %get-tuple-element.134), channel_id=1, source_target_pairs={{2,0},{3,1},{6,4},{7,5},{10,8},{11,9},{14,12},{15,13},{18,16},{19,... | collective-permute-start | bytes 196616 | tf_op jit(solution)/shard_map/ppermute | solution.py:25
  121.2 36.5 %collective-permute-start.22 = (f32[2,1,32,256]{3,2,1,0:T(8,128)S(1)}, f32[2,1,32,256]{3,2,1,0:T(8,128)S(1)}, u32[]{:S(2)}, u32[]{:S(2)}) collective-permute-start(f32[2,1,32,256]{3,2,1,0:T(8,128)S(1)} %get-tuple-element.133), channel_id=1, source_target_pairs={{0,2},{1,3},{4,6},{5,7},{8,10},{9,11},{12,14},{13,15},{16,18},{17,... | collective-permute-start | bytes 196616 | tf_op jit(solution)/shard_map/ppermute | solution.py:23
  127.1 4.9 %collective-permute-start.26 = (f32[4,1,256]{2,0,1:T(4,128)S(1)}, f32[4,1,256]{2,0,1:T(4,128)S(1)}, u32[]{:S(2)}, u32[]{:S(2)}) collective-permute-start(f32[4,1,256]{2,0,1:T(4,128)S(1)} %collective-permute-done.25), channel_id=1, source_target_pairs={{0,1},{1,4},{4,5},{5,8},{8,9},{9,12},{12,13},{13,0},{2,3},{3,6},{6... | collective-permute-start | bytes 12296 | tf_op jit(solution)/shard_map/ppermute | solution.py:56
  158.0 61.7 %collective-permute-start.32 = (f32[2,6,1,256]{3,1,2,0:T(8,128)S(1)}, f32[2,6,1,256]{3,1,2,0:T(8,128)S(1)}, u32[]{:S(2)}, u32[]{:S(2)}) collective-permute-start(f32[2,6,1,256]{3,1,2,0:T(8,128)S(1)} %slice.192), channel_id=1, source_target_pairs={{0,1},{2,3},{4,5},{6,7},{8,9},{10,11},{12,13},{14,15},{16,17},{18,... | collective-permute-start | bytes 36872 | tf_op jit(solution)/shard_map/ppermute | solution.py:23
  160.2 13.8 %collective-permute-start.24 = (f32[2,6,1,256]{1,3,2,0:T(8,128)}, f32[2,6,1,256]{1,3,2,0:T(8,128)}, u32[]{:S(2)}, u32[]{:S(2)}) collective-permute-start(f32[2,6,1,256]{1,3,2,0:T(8,128)} %copy.292), channel_id=1, source_target_pairs={{1,0},{3,2},{5,4},{7,6},{9,8},{11,10},{13,12},{15,14},{17,16},{19,... | collective-permute-start | bytes 36872 | tf_op jit(solution)/shard_map/ppermute | solution.py:25
  170.6 40.4 %all-to-all-start.2 = ((f32[4,1,8192]{2,1,0:T(1,128)}), f32[4,1,8192]{2,1,0:T(1,128)S(1)}, u32[]{:S(2)}, u32[]{:S(2)}) async-start(f32[4,1,8192]{2,1,0:T(1,128)} %reshape.118), calls=%async_computation.2 | async-start | bytes 262144 | tf_op jit(solution)/shard_map/all_to_all | solution.py:164
  222.9 11.6 %collective-permute-start.36 = (f32[4,1,256]{2,0,1:T(4,128)S(1)}, f32[4,1,256]{2,0,1:T(4,128)S(1)}, u32[]{:S(2)}, u32[]{:S(2)}) collective-permute-start(f32[4,1,256]{2,0,1:T(4,128)S(1)} %get-tuple-element.143), channel_id=1, source_target_pairs={{0,1},{1,4},{4,5},{5,8},{8,9},{9,12},{12,13},{13,0},{2,3},{3,6},{6... | collective-permute-start | bytes 12296 | tf_op jit(solution)/shard_map/ppermute | solution.py:56
  223.0 52.1 %all-to-all-start.3 = ((f32[4,32,256]{2,0,1:T(4,128)}), f32[4,32,256]{2,0,1:T(4,128)S(1)}, u32[]{:S(2)}, u32[]{:S(2)}) async-start(f32[4,32,256]{2,0,1:T(4,128)} %multiply_subtract_fusion.1), calls=%async_computation.3 | async-start | bytes 262144 | tf_op jit(solution)/shard_map/all_to_all | solution.py:182
  227.3 37.8 %collective-permute-start.34 = (f32[2,1,32,256]{3,2,1,0:T(8,128)S(1)}, f32[2,1,32,256]{3,2,1,0:T(8,128)S(1)}, u32[]{:S(2)}, u32[]{:S(2)}) collective-permute-start(f32[2,1,32,256]{3,2,1,0:T(8,128)S(1)} %get-tuple-element.130), channel_id=1, source_target_pairs={{2,0},{3,1},{6,4},{7,5},{10,8},{11,9},{14,12},{15,13},{18,16},{19,... | collective-permute-start | bytes 196616 | tf_op jit(solution)/shard_map/ppermute | solution.py:25
  228.6 36.5 %collective-permute-start.33 = (f32[2,1,32,256]{3,2,1,0:T(8,128)S(1)}, f32[2,1,32,256]{3,2,1,0:T(8,128)S(1)}, u32[]{:S(2)}, u32[]{:S(2)}) collective-permute-start(f32[2,1,32,256]{3,2,1,0:T(8,128)S(1)} %get-tuple-element.129), channel_id=1, source_target_pairs={{0,2},{1,3},{4,6},{5,7},{8,10},{9,11},{12,14},{13,15},{16,18},{17,... | collective-permute-start | bytes 196616 | tf_op jit(solution)/shard_map/ppermute | solution.py:23
  234.5 5.5 %collective-permute-start.37 = (f32[4,1,256]{2,0,1:T(4,128)S(1)}, f32[4,1,256]{2,0,1:T(4,128)S(1)}, u32[]{:S(2)}, u32[]{:S(2)}) collective-permute-start(f32[4,1,256]{2,0,1:T(4,128)S(1)} %collective-permute-done.36), channel_id=1, source_target_pairs={{0,1},{1,4},{4,5},{5,8},{8,9},{9,12},{12,13},{13,0},{2,3},{3,6},{6... | collective-permute-start | bytes 12296 | tf_op jit(solution)/shard_map/ppermute | solution.py:56
  265.5 5.8 %collective-permute-start.43 = (f32[2,6,1,256]{3,1,2,0:T(8,128)S(1)}, f32[2,6,1,256]{3,1,2,0:T(8,128)S(1)}, u32[]{:S(2)}, u32[]{:S(2)}) collective-permute-start(f32[2,6,1,256]{3,1,2,0:T(8,128)S(1)} %slice.200), channel_id=1, source_target_pairs={{1,0},{3,2},{5,4},{7,6},{9,8},{11,10},{13,12},{15,14},{17,16},{19,... | collective-permute-start | bytes 36872 | tf_op jit(solution)/shard_map/ppermute | solution.py:25
  (40 other events, 414.8 us)
